TPU v7x, 256 devices: a whole 4x4x8 slice. The times are simulated.
256 devices in a mesh: node: 16 (over x, y), feat: 16 (over z, core).
Axes of the slice: x: 4, y: 4, z: 8, core: 2. Of those that a mesh axis runs over, the one named last changes fastest.
Arguments:
- feats_t: float32 [512, 16384], P('feat', 'node'), may hold values from -6 to 6
- weight: float32 [512, 512], P(None, 'feat'), may hold values from -0.25 to 0.25
- cot_t: float32 [512, 16384], P('feat', 'node'), may hold values from -6 to 6
- tiles: float32 [128, 8, 128, 128], P('node'), may hold values from -0.1875 to 0.1875
- col_ids: int32 [128, 8], P('node'), may hold values from 0 to 127, as said below
- counts: int32 [128], P('node'), may hold values from 1 to 8, as said below
Outputs:
- out_t: float32 [512, 16384], P('feat', 'node')
- grad_feats: float32 [512, 16384], P('feat', 'node')
- grad_weight: float32 [512, 512], P(None, 'feat')
Inputs may be any that keep to these rules, and one draw needn't show every extreme that they name: `col_ids`: column block c belongs to node index c // 8. Among the 64 slots of one node index's row blocks, at most 4 name column blocks of any one node index, and some node index is named by exactly 4; ids may repeat within a row block. `counts`: row block 0 has all 8 slots live; loads differ between devices.
All inputs are finite; a program needn't handle non-finite values.
Results may differ from a plain program's by a relative error of at most 0.0001.
Values sent between devices are 32-bit elements; how exact they have to be, the bound alone decides.
A program may use at most 64 MiB of HBM per device.

v0:
```python
import jax
import jax.numpy as jnp
from jax import lax
from jax.sharding import PartitionSpec as P

HIGH = lax.Precision.HIGHEST


def from_root(value, axis, source):
    kept = jnp.where(lax.axis_index(axis) == source, value, 0).astype(value.dtype)
    return lax.psum(kept, axis)


def on_device(feats_t, weight, cot_t, tiles, col_ids, counts):
    width_part, rows = feats_t.shape
    nblocks = tiles.shape[0]
    slots = tiles.shape[1]
    local_blocks = rows // 128
    node_count = lax.axis_size("node")
    total = local_blocks * node_count
    live = (jnp.arange(slots)[None, :] < counts[:, None]).astype(jnp.float32)
    empty = jnp.zeros((width_part, nblocks, slots, 128), jnp.float32)
    owner = col_ids // local_blocks
    within = col_ids % local_blocks

    def section(root, selected):
        received = from_root(feats_t, "node", root)
        shaped = received.reshape(width_part, local_blocks, 128)
        picked = jnp.take(shaped, within, axis=1)
        return jnp.where((owner == root)[None, :, :, None], picked, selected)

    selected = lax.fori_loop(0, node_count, section, empty)
    selected = selected * live[None, :, :, None]
    mixed_t = jnp.einsum("fbkc,bkrc->fbr", selected, tiles, precision=HIGH).reshape(
        width_part, rows
    )
    mixed_full = lax.all_gather(mixed_t, "feat", axis=0, tiled=True)
    pre_t = jnp.dot(weight.T, mixed_full, precision=HIGH)
    sig = jax.nn.sigmoid(pre_t)
    out_t = pre_t * sig
    grad_pre = cot_t * (sig * (1.0 + pre_t * (1.0 - sig)))
    grad_weight = lax.psum(jnp.dot(mixed_full, grad_pre.T, precision=HIGH), "node")
    grad_mixed = lax.psum_scatter(
        jnp.dot(weight, grad_pre, precision=HIGH), "feat", scatter_dimension=0, tiled=True
    )
    contrib = jnp.einsum(
        "fbr,bkrc->fbkc", grad_mixed.reshape(width_part, nblocks, 128), tiles, precision=HIGH
    )
    contrib = contrib * live[None, :, :, None]
    onehot = (col_ids[:, :, None] == jnp.arange(total)[None, None, :]).astype(jnp.float32)
    partial_grad = jnp.einsum("fbkc,bkj->fjc", contrib, onehot, precision=HIGH).reshape(
        width_part, total * 128
    )
    grad_feats = lax.psum_scatter(partial_grad, "node", scatter_dimension=1, tiled=True)
    return (out_t, grad_feats, grad_weight)


def solution(mesh):
    return jax.shard_map(
        on_device,
        mesh=mesh,
        in_specs=(
            P("feat", "node"),
            P(None, "feat"),
            P("feat", "node"),
            P("node", None, None, None),
            P("node", None),
            P("node"),
        ),
        out_specs=(P("feat", "node"), P("feat", "node"), P(None, "feat")),
        check_vma=False,
    )
```

profile of v0, /device:TPU:2, one launch (start us, length us, event | category | flops | bytes accessed | tf_op | source)
XLA Modules:
  0.0 1878.7 jit_solution(987238460676156024)
XLA Ops:
  9.5 1572.9 %while.16 = (s32[]{:T(128)}, f32[32,8,8,128]{3,0,2,1:T(8,128)S(1)}, s32[8,8]{1,0:T(8,128)S(1)}, s32[8,8]{1,0:T(8,128)S(1)}, f32[32,1024]{1,0:T(8,128)}, /*index=5*/s32[]{:T(128)}, u32[]{:T(128)}, u32[]{:T(128)}, s32[]{:T(128)}) while((s32[]{:T(128)}, f32[32,8,8,128]{3,0,2,1:T(8,128)S(1)}, s32[8,8]{1,0:T(8,128)S(1)}, ...), condition=%wide.region_2.3_spmd.clone, body=%wide.region_0.2_spmd.clone.sunk | while | flops 853639 | bytes 6298053 | solution.py:32
  10.4 98.7 %all-reduce.5.cloned.1.call-done = f32[32,8,128]{2,0,1:T(8,128)} async-done(((f32[32,8,128]{2,0,1:T(8,128)}), f32[32,8,128]{2,0,1:T(8,128)}) %all-reduce.5.cloned.1.call-update) | async-done | bytes 131088 | tf_op jit(solution)/shard_map/while/body/eval_jaxpr/psum | solution.py:11
  111.8 95.5 %all-reduce.5.cloned.1.call-done = f32[32,8,128]{2,0,1:T(8,128)} async-done(((f32[32,8,128]{2,0,1:T(8,128)}), f32[32,8,128]{2,0,1:T(8,128)}) %all-reduce.5.cloned.1.call-update) | async-done | bytes 131088 | tf_op jit(solution)/shard_map/while/body/eval_jaxpr/psum | solution.py:11
  210.1 95.5 %all-reduce.5.cloned.1.call-done = f32[32,8,128]{2,0,1:T(8,128)} async-done(((f32[32,8,128]{2,0,1:T(8,128)}), f32[32,8,128]{2,0,1:T(8,128)}) %all-reduce.5.cloned.1.call-update) | async-done | bytes 131088 | tf_op jit(solution)/shard_map/while/body/eval_jaxpr/psum | solution.py:11
  308.3 95.2 %all-reduce.5.cloned.1.call-done = f32[32,8,128]{2,0,1:T(8,128)} async-done(((f32[32,8,128]{2,0,1:T(8,128)}), f32[32,8,128]{2,0,1:T(8,128)}) %all-reduce.5.cloned.1.call-update) | async-done | bytes 131088 | tf_op jit(solution)/shard_map/while/body/eval_jaxpr/psum | solution.py:11
  407.2 94.3 %all-reduce.5.cloned.1.call-done = f32[32,8,128]{2,0,1:T(8,128)} async-done(((f32[32,8,128]{2,0,1:T(8,128)}), f32[32,8,128]{2,0,1:T(8,128)}) %all-reduce.5.cloned.1.call-update) | async-done | bytes 131088 | tf_op jit(solution)/shard_map/while/body/eval_jaxpr/psum | solution.py:11
  504.2 95.2 %all-reduce.5.cloned.1.call-done = f32[32,8,128]{2,0,1:T(8,128)} async-done(((f32[32,8,128]{2,0,1:T(8,128)}), f32[32,8,128]{2,0,1:T(8,128)}) %all-reduce.5.cloned.1.call-update) | async-done | bytes 131088 | tf_op jit(solution)/shard_map/while/body/eval_jaxpr/psum | solution.py:11
  602.2 95.5 %all-reduce.5.cloned.1.call-done = f32[32,8,128]{2,0,1:T(8,128)} async-done(((f32[32,8,128]{2,0,1:T(8,128)}), f32[32,8,128]{2,0,1:T(8,128)}) %all-reduce.5.cloned.1.call-update) | async-done | bytes 131088 | tf_op jit(solution)/shard_map/while/body/eval_jaxpr/psum | solution.py:11
  700.5 95.5 %all-reduce.5.cloned.1.call-done = f32[32,8,128]{2,0,1:T(8,128)} async-done(((f32[32,8,128]{2,0,1:T(8,128)}), f32[32,8,128]{2,0,1:T(8,128)}) %all-reduce.5.cloned.1.call-update) | async-done | bytes 131088 | tf_op jit(solution)/shard_map/while/body/eval_jaxpr/psum | solution.py:11
  798.7 95.5 %all-reduce.5.cloned.1.call-done = f32[32,8,128]{2,0,1:T(8,128)} async-done(((f32[32,8,128]{2,0,1:T(8,128)}), f32[32,8,128]{2,0,1:T(8,128)}) %all-reduce.5.cloned.1.call-update) | async-done | bytes 131088 | tf_op jit(solution)/shard_map/while/body/eval_jaxpr/psum | solution.py:11
  897.0 95.2 %all-reduce.5.cloned.1.call-done = f32[32,8,128]{2,0,1:T(8,128)} async-done(((f32[32,8,128]{2,0,1:T(8,128)}), f32[32,8,128]{2,0,1:T(8,128)}) %all-reduce.5.cloned.1.call-update) | async-done | bytes 131088 | tf_op jit(solution)/shard_map/while/body/eval_jaxpr/psum | solution.py:11
  994.9 95.5 %all-reduce.5.cloned.1.call-done = f32[32,8,128]{2,0,1:T(8,128)} async-done(((f32[32,8,128]{2,0,1:T(8,128)}), f32[32,8,128]{2,0,1:T(8,128)}) %all-reduce.5.cloned.1.call-update) | async-done | bytes 131088 | tf_op jit(solution)/shard_map/while/body/eval_jaxpr/psum | solution.py:11
  1093.2 95.2 %all-reduce.5.cloned.1.call-done = f32[32,8,128]{2,0,1:T(8,128)} async-done(((f32[32,8,128]{2,0,1:T(8,128)}), f32[32,8,128]{2,0,1:T(8,128)}) %all-reduce.5.cloned.1.call-update) | async-done | bytes 131088 | tf_op jit(solution)/shard_map/while/body/eval_jaxpr/psum | solution.py:11
  1191.1 95.5 %all-reduce.5.cloned.1.call-done = f32[32,8,128]{2,0,1:T(8,128)} async-done(((f32[32,8,128]{2,0,1:T(8,128)}), f32[32,8,128]{2,0,1:T(8,128)}) %all-reduce.5.cloned.1.call-update) | async-done | bytes 131088 | tf_op jit(solution)/shard_map/while/body/eval_jaxpr/psum | solution.py:11
  1289.4 95.2 %all-reduce.5.cloned.1.call-done = f32[32,8,128]{2,0,1:T(8,128)} async-done(((f32[32,8,128]{2,0,1:T(8,128)}), f32[32,8,128]{2,0,1:T(8,128)}) %all-reduce.5.cloned.1.call-update) | async-done | bytes 131088 | tf_op jit(solution)/shard_map/while/body/eval_jaxpr/psum | solution.py:11
  1387.3 95.2 %all-reduce.5.cloned.1.call-done = f32[32,8,128]{2,0,1:T(8,128)} async-done(((f32[32,8,128]{2,0,1:T(8,128)}), f32[32,8,128]{2,0,1:T(8,128)}) %all-reduce.5.cloned.1.call-update) | async-done | bytes 131088 | tf_op jit(solution)/shard_map/while/body/eval_jaxpr/psum | solution.py:11
  1485.3 95.2 %all-reduce.5.cloned.1.call-done = f32[32,8,128]{2,0,1:T(8,128)} async-done(((f32[32,8,128]{2,0,1:T(8,128)}), f32[32,8,128]{2,0,1:T(8,128)}) %all-reduce.5.cloned.1.call-update) | async-done | bytes 131088 | tf_op jit(solution)/shard_map/while/body/eval_jaxpr/psum | solution.py:11
  1582.4 6.1 convolution_bitcast_fusion.1
  1589.3 39.5 %all-gather.2.cloned.1.call-done = f32[512,1024]{1,0:T(8,128)} async-done(((f32[32,1024]{1,0:T(8,128)}), f32[512,1024]{1,0:T(8,128)}) %all-gather.2.cloned.1.call-update) | async-done | bytes 2097168 | tf_op jit(solution)/shard_map/all_gather | solution.py:37
  1628.8 3.6 fusion.5
  1640.5 53.4 %reduce-scatter.7.cloned.1.call-done = f32[32,1024]{1,0:T(8,128)} async-done(((f32[512,1024]{1,0:T(8,128)}), f32[32,1024]{1,0:T(8,128)}) %reduce-scatter.7.cloned.1.call-update) | async-done | bytes 131088
  1695.0 3.9 fusion
  1703.2 83.2 %all-reduce.3.cloned.1.call-done = f32[512,32]{0,1:T(8,128)} async-done(((f32[512,32]{0,1:T(8,128)}), f32[512,32]{0,1:T(8,128)}) %all-reduce.3.cloned.1.call-update) | async-done | bytes 65552 | tf_op jit(solution)/shard_map/psum | solution.py:42
  1786.4 83.4 %reduce-scatter.5.cloned.1.call-done = f32[32,1024]{1,0:T(8,128)} async-done(((f32[32,16384]{1,0:T(8,128)}), f32[32,1024]{1,0:T(8,128)}) %reduce-scatter.5.cloned.1.call-update) | async-done | bytes 131088 | tf_op jit(solution)/shard_map/reduce_scatter | solution.py:54
  (171 shorter events, 60.5 us)
Async XLA Ops:
  8.0 1620.8 %copy-start = (f32[512,32]{0,1:T(8,128)S(1)}, f32[512,32]{0,1:T(8,128)}, u32[]{:S(2)}) copy-start(f32[512,32]{0,1:T(8,128)} %param.9) | copy-start | bytes 196612
  9.5 99.6 %all-reduce.5.cloned.1.call-start = ((), (), s32[]{:S(2)}) async-start(), calls=%async_computation.6 | async-start | bytes 262144 | tf_op jit(solution)/shard_map/while/body/eval_jaxpr/psum | solution.py:11
  110.9 96.4 %all-reduce.5.cloned.1.call-start = ((), (), s32[]{:S(2)}) async-start(), calls=%async_computation.6 | async-start | bytes 262144 | tf_op jit(solution)/shard_map/while/body/eval_jaxpr/psum | solution.py:11
  209.2 96.4 %all-reduce.5.cloned.1.call-start = ((), (), s32[]{:S(2)}) async-start(), calls=%async_computation.6 | async-start | bytes 262144 | tf_op jit(solution)/shard_map/while/body/eval_jaxpr/psum | solution.py:11
  307.4 96.1 %all-reduce.5.cloned.1.call-start = ((), (), s32[]{:S(2)}) async-start(), calls=%async_computation.6 | async-start | bytes 262144 | tf_op jit(solution)/shard_map/while/body/eval_jaxpr/psum | solution.py:11
  405.4 96.1 %all-reduce.5.cloned.1.call-start = ((), (), s32[]{:S(2)}) async-start(), calls=%async_computation.6 | async-start | bytes 262144 | tf_op jit(solution)/shard_map/while/body/eval_jaxpr/psum | solution.py:11
  503.4 96.1 %all-reduce.5.cloned.1.call-start = ((), (), s32[]{:S(2)}) async-start(), calls=%async_computation.6 | async-start | bytes 262144 | tf_op jit(solution)/shard_map/while/body/eval_jaxpr/psum | solution.py:11
  601.3 96.4 %all-reduce.5.cloned.1.call-start = ((), (), s32[]{:S(2)}) async-start(), calls=%async_computation.6 | async-start | bytes 262144 | tf_op jit(solution)/shard_map/while/body/eval_jaxpr/psum | solution.py:11
  699.6 96.4 %all-reduce.5.cloned.1.call-start = ((), (), s32[]{:S(2)}) async-start(), calls=%async_computation.6 | async-start | bytes 262144 | tf_op jit(solution)/shard_map/while/body/eval_jaxpr/psum | solution.py:11
  797.8 96.4 %all-reduce.5.cloned.1.call-start = ((), (), s32[]{:S(2)}) async-start(), calls=%async_computation.6 | async-start | bytes 262144 | tf_op jit(solution)/shard_map/while/body/eval_jaxpr/psum | solution.py:11
  896.1 96.1 %all-reduce.5.cloned.1.call-start = ((), (), s32[]{:S(2)}) async-start(), calls=%async_computation.6 | async-start | bytes 262144 | tf_op jit(solution)/shard_map/while/body/eval_jaxpr/psum | solution.py:11
  994.0 96.4 %all-reduce.5.cloned.1.call-start = ((), (), s32[]{:S(2)}) async-start(), calls=%async_computation.6 | async-start | bytes 262144 | tf_op jit(solution)/shard_map/while/body/eval_jaxpr/psum | solution.py:11
  1092.3 96.1 %all-reduce.5.cloned.1.call-start = ((), (), s32[]{:S(2)}) async-start(), calls=%async_computation.6 | async-start | bytes 262144 | tf_op jit(solution)/shard_map/while/body/eval_jaxpr/psum | solution.py:11
  1190.2 96.4 %all-reduce.5.cloned.1.call-start = ((), (), s32[]{:S(2)}) async-start(), calls=%async_computation.6 | async-start | bytes 262144 | tf_op jit(solution)/shard_map/while/body/eval_jaxpr/psum | solution.py:11
  1288.5 96.1 %all-reduce.5.cloned.1.call-start = ((), (), s32[]{:S(2)}) async-start(), calls=%async_computation.6 | async-start | bytes 262144 | tf_op jit(solution)/shard_map/while/body/eval_jaxpr/psum | solution.py:11
  1386.5 96.1 %all-reduce.5.cloned.1.call-start = ((), (), s32[]{:S(2)}) async-start(), calls=%async_computation.6 | async-start | bytes 262144 | tf_op jit(solution)/shard_map/while/body/eval_jaxpr/psum | solution.py:11
  1484.4 96.1 %all-reduce.5.cloned.1.call-start = ((), (), s32[]{:S(2)}) async-start(), calls=%async_computation.6 | async-start | bytes 262144 | tf_op jit(solution)/shard_map/while/body/eval_jaxpr/psum | solution.py:11
  1582.4 46.4 %all-gather.2.cloned.1.call-start = ((), (), s32[]{:S(2)}) async-start(), calls=%async_computation.2 | async-start | bytes 2228224 | tf_op jit(solution)/shard_map/all_gather | solution.py:37
  1588.5 43.9 %copy-start.2 = (f32[32,1024]{1,0:T(8,128)S(1)}, f32[32,1024]{1,0:T(8,128)}, u32[]{:S(2)}) copy-start(f32[32,1024]{1,0:T(8,128)} %param.10) | copy-start | bytes 393220
  1589.2 104.7 %reduce-scatter.7.cloned.1.call-start = ((), (), s32[]{:S(2)}) async-start(), calls=%async_computation.5 | async-start | bytes 2228224
  1636.1 1.6 copy-start.1
  1636.1 150.3 %all-reduce.3.cloned.1.call-start = ((), (), s32[]{:S(2)}) async-start(), calls=%async_computation.4 | async-start | bytes 131072 | tf_op jit(solution)/shard_map/psum | solution.py:42
  1640.4 229.4 %reduce-scatter.5.cloned.1.call-start = ((), (), s32[]{:S(2)}) async-start(), calls=%async_computation.3 | async-start | bytes 2228224 | tf_op jit(solution)/shard_map/reduce_scatter | solution.py:54
  1695.0 3.9 copy-start.3
Sparse Core Ops, SparseCore 0:
  14.1 94.9 all-reduce.4
  115.6 91.7 all-reduce.4
  213.8 91.7 all-reduce.4
  311.7 91.7 all-reduce.4
  409.7 91.7 all-reduce.4
  507.7 91.7 all-reduce.4
  605.9 91.7 all-reduce.4
  704.2 91.7 all-reduce.4
  802.4 91.7 all-reduce.4
  900.4 91.7 all-reduce.4
  998.6 91.7 all-reduce.4
  1096.6 91.7 all-reduce.4
  1194.9 91.7 all-reduce.4
  1292.8 91.7 all-reduce.4
  1390.8 91.7 all-reduce.4
  1488.7 91.7 all-reduce.4
Sparse Core Ops, SparseCore 1:
  1589.3 39.4 all-gather.1
  1636.2 57.6 reduce-scatter.6
  1697.5 88.9 all-reduce.2
  1791.0 78.8 reduce-scatter.4
where the time goes:
time: 1880 us
  waiting for transfers between devices  1790 us (95%)
  local copies, waits for them, and re-layouts  34.7 us (2%)
  matrix products  19.9 us (1%)
    psum x16, waiting for transfers between devices, from_root(): return lax.psum(kept, axis)  1530 us
    reduce_scatter x1, waiting for transfers between devices, on_device(): lax.psum_scatter(partial_grad, 'node', scatter_dimension=1, tiled=True)  83.4 us
    psum x1, waiting for transfers between devices, on_device(): lax.psum(jnp.dot(mixed_full, grad_pre.T, precision=HIGH), 'node')  83.2 us
    unnamed x5, waiting for transfers between devices  53.5 us
    all_gather x1, waiting for transfers between devices, on_device(): mixed_full = lax.all_gather(mixed_t, 'feat', axis=0, tiled=True)  39.5 us
  transfers between devices with their start and end apart: 20, of which 20 were waited for; matrix products, arithmetic and copies ran while one was open for 1% of the time, Pallas kernels for 0%

commit v1 on v0

v1 whole, which is shorter than its diff:
```python
import jax
import jax.numpy as jnp
from jax import lax
from jax.experimental import pallas as pl
from jax.experimental.pallas import tpu as pltpu
from jax.sharding import PartitionSpec as P

MESH = pl.DeviceIdType.MESH
F32 = jnp.float32
BF16 = jnp.bfloat16
I32 = jnp.int32
NN = (((1,), (0,)), ((), ()))
NT = (((1,), (1,)), ((), ()))
FAR = (4, 3, 5, 2, 6, 1, 7)


def split(v):
    hi = v.astype(BF16)
    return hi, (v - hi.astype(F32)).astype(BF16)


def mm(a, b, dims):
    return lax.dot_general(a, b, dims, preferred_element_type=F32)


def kernel(
    feats, wt, cot, tiles, cols_h, counts_h,
    out, gf, gwt,
    t32, tb, f3, av0, av1, sv, rv, mx, mv, wa, wst, wn, ca,
    oo, orv, pv, px, gs, gv, gwp, gwr, gw0, gwa, gw1, gwb,
    cv, sb, qv, dv, ev, tab, tabr, tabs, tabrs, cols, counts,
    sem_t, sem_s, sem_i,
    s1, r1, s1t, r1t, s2, r2, sw, rw, sc, rc, sm, rm, sf, rf, sp, rp,
    so, ro, sg, rg, sgw, rgw, sq, rq, se, re, sga, rga, sgb, rgb,
):
    node = lax.axis_index("node")
    feat = lax.axis_index("feat")
    x, y = lax.div(node, 4), lax.rem(node, 4)
    z, c = lax.div(feat, 2), lax.rem(feat, 2)
    oc = 1 - c

    def at_x(d):
        return lax.rem(x + d, 4)

    def at_y(d):
        return lax.rem(y + d, 4)

    def at_z(d):
        return lax.rem(z + d, 8)

    def xdev(d):
        return (at_x(d) * 4 + y, feat)

    def ydev(d):
        return (x * 4 + at_y(d), feat)

    def zdev(d):
        return (node, at_z(d) * 2 + c)

    cdev = (node, z * 2 + oc)
    pending = []

    def send(src, dst, device, ss, rs):
        cp = pltpu.make_async_remote_copy(
            src_ref=src, dst_ref=dst, send_sem=ss, recv_sem=rs,
            device_id=device, device_id_type=MESH,
        )
        cp.start()
        pending.append(cp)
        return cp

    ids = [
        pltpu.make_async_copy(cols_h, cols, sem_i.at[0]),
        pltpu.make_async_copy(counts_h, counts, sem_i.at[1]),
    ]
    fcopies = [
        pltpu.make_async_copy(feats.at[:, pl.ds(128 * w, 128)], f3.at[w], sem_i.at[2 + w])
        for w in range(8)
    ]
    own = [
        pltpu.make_async_copy(wt, wa.at[z], sem_i.at[10]),
        pltpu.make_async_copy(cot.at[:, pl.ds(pl.multiple_of(z * 128, 128), 128)], ca.at[z], sem_i.at[11]),
    ]
    for cp in ids + fcopies + own:
        cp.start()
    for b in range(8):
        pltpu.make_async_copy(tiles.at[b], t32.at[b], sem_t.at[b]).start()
    barrier = pltpu.get_barrier_semaphore()
    peers = [xdev(d) for d in (1, 2, 3)] + [ydev(d) for d in (1, 2, 3)]
    peers += [zdev(d) for d in range(1, 8)] + [cdev]
    for p in peers:
        pl.semaphore_signal(barrier, 1, device_id=p, device_id_type=MESH)

    for cp in ids:
        cp.wait()
    lane8 = lax.broadcasted_iota(I32, (8, 128), 1)
    sub8 = lax.broadcasted_iota(I32, (8, 128), 0)
    by_lane = jnp.full((8, 128), 1024, I32)
    for s in range(64):
        by_lane = jnp.where(lane8 == s, cols[s // 8, s % 8], by_lane)
    place_l = jnp.zeros((8, 128), I32)
    rows = []
    for g in range(8):
        by_sub = jnp.zeros((8, 128), I32)
        for k in range(8):
            by_sub = jnp.where(sub8 == k, cols[g, k], by_sub)
        rows.append(by_sub)
    own_l = lax.shift_right_logical(by_lane, 3)
    slot_sum = jnp.zeros((8, 128), I32)
    want_sum = jnp.zeros((8, 128), I32)
    for g in range(8):
        own_s = lax.shift_right_logical(rows[g], 3)
        slot_s = sub8 + 8 * g
        same = own_s == own_l
        place_l = place_l + jnp.where(same & (slot_s < lane8), 1, 0)
        rank = jnp.sum(jnp.where(same & (lane8 < slot_s), 1, 0), axis=1, keepdims=True)
        hit = (own_s * 4 + rank) == lane8
        slot_sum = slot_sum + jnp.where(hit, slot_s, 0)
        want_sum = want_sum + jnp.where(hit, rows[g] & 7, 0)
    place = own_l * 4 + jnp.sum(place_l, axis=0, keepdims=True)
    slot_of = jnp.sum(slot_sum, axis=0, keepdims=True)
    want = jnp.sum(want_sum, axis=0, keepdims=True)
    table = jnp.where(sub8 == 0, place, jnp.where(sub8 == 1, slot_of, want))
    tab[...] = table
    tabr[0, y] = table
    tabr[1, x] = table

    for cp in fcopies:
        cp.wait()
    av0[x] = f3[:, 0:16]
    av1[y] = f3[:, 16:32]
    pl.semaphore_wait(barrier, len(peers))

    tx = [send(tab, tabr.at[1, x], xdev(d), s1t.at[0, d], r1t.at[0, d]) for d in (1, 2, 3)]
    ty = [send(tab, tabr.at[0, y], ydev(d), s1t.at[1, d], r1t.at[1, d]) for d in (1, 2, 3)]
    fx = [send(f3.at[:, pl.ds(0, 16)], av0.at[x], xdev(d), s1.at[0, d], r1.at[0, d]) for d in (2, 1, 3)]
    fy = [send(f3.at[:, pl.ds(16, 16)], av1.at[y], ydev(d), s1.at[1, d], r1.at[1, d]) for d in (2, 1, 3)]
    cz = [send(cot.at[:, pl.ds(pl.multiple_of(at_z(d) * 128, 128), 128)], ca.at[z], zdev(d), sc.at[d], rc.at[d]) for d in FAR]
    wz = [send(wt, wa.at[z], zdev(d), sw.at[d], rw.at[d]) for d in FAR]
    to_s = pltpu.make_async_copy(tab, tabs, sem_s.at[0])
    to_s.start()

    def convert(b, carry):
        pltpu.make_async_copy(tiles.at[b], t32.at[b], sem_t.at[b]).wait()
        for k in range(8):
            live = jnp.where(k < counts[b], 1.0, 0.0).astype(F32)
            hi, lo = split(t32[b, k] * live)
            q = 128 * (k % 2)
            tb[b, k // 2, 0:128, q : q + 128] = hi
            tb[b, k // 2, 128:256, q : q + 128] = lo
        return carry

    lax.fori_loop(0, 8, convert, 0)

    to_s.wait()
    for cp in tx + ty:
        cp.wait_recv()
    to_rs = pltpu.make_async_copy(tabr, tabrs, sem_s.at[1])
    to_rs.start()
    to_rs.wait()

    for cp in fx:
        cp.wait_recv()
    leg2 = []
    for d in (2, 1, 3, 0):
        yd = at_y(d)
        for xo in range(4):
            for r in range(4):
                w = tabrs[0, yd, 2, (xo * 4 + y) * 4 + r]
                block = av0[xo, w]
                if d:
                    sv[0, d, xo, r] = block
                else:
                    rv[xo, y, r, 0:16] = block
        if d:
            leg2.append(
                send(sv.at[0, d], rv.at[:, y, :, pl.ds(0, 16)], ydev(d), s2.at[0, d], r2.at[0, d])
            )
    for cp in fy:
        cp.wait_recv()
    for d in (2, 1, 3, 0):
        xd = at_x(d)
        for yo in range(4):
            for r in range(4):
                w = tabrs[1, xd, 2, (x * 4 + yo) * 4 + r]
                block = av1[yo, w]
                if d:
                    sv[1, d, yo, r] = block
                else:
                    rv[x, yo, r, 16:32] = block
        if d:
            leg2.append(
                send(sv.at[1, d], rv.at[x, :, :, pl.ds(16, 16)], xdev(d), s2.at[1, d], r2.at[1, d])
            )

    for cp in wz:
        cp.wait_recv()
    for cp in own:
        cp.wait()
    for q in range(8):
        hi, lo = split(wa[q])
        wst[32 * q : 32 * q + 32] = hi
        wst[256 + 32 * q : 288 + 32 * q] = lo
    for g in range(4):
        turned = jnp.transpose(wa[:, :, 128 * g : 128 * g + 128].reshape(256, 128))
        hi, lo = split(turned)
        wn[128 * g : 128 * g + 128] = hi
        wn[512 + 128 * g : 640 + 128 * g] = lo

    for cp in leg2:
        cp.wait_recv()

    mz = []
    for d in FAR + (0,):
        b = at_z(d)
        acc = None
        for kp in range(4):
            parts = []
            for k in (2 * kp, 2 * kp + 1):
                p = tabs[0, b * 8 + k]
                parts.append(
                    split(rv[lax.shift_right_logical(p, 4), lax.shift_right_logical(p, 2) & 3, p & 3])
                )
            lhs = jnp.concatenate(
                [
                    jnp.concatenate([parts[0][0], parts[1][0]], axis=1),
                    jnp.concatenate([parts[0][1], parts[1][1]], axis=1),
                ],
                axis=0,
            )
            term = mm(lhs, tb[b, kp], NT)
            acc = term if acc is None else acc + term
        mixed = (acc[32:64, 128:256] + acc[32:64, 0:128] + acc[0:32, 128:256]) + acc[0:32, 0:128]
        if d:
            mx[d] = mixed
            mz.append(send(mx.at[d], mv.at[z, c], zdev(d), sm.at[d], rm.at[d]))
        else:
            mv[z, c] = mixed
    fz = [send(mv.at[z, c], mv.at[z, c], cdev, sf.at[0], rf.at[0])]
    for i, d in enumerate(FAR):
        mz[i].wait_recv()
        q = at_z(8 - d)
        fz.append(send(mv.at[q, c], mv.at[q, c], cdev, sf.at[d], rf.at[d]))
    for cp in cz:
        cp.wait_recv()
    for cp in fz:
        cp.wait_recv()

    hi, lo = split(mv[...].reshape(512, 128))
    mhl = jnp.concatenate([hi, lo], axis=1)
    r = mm(wst[...], mhl, NN)
    pre = (r[256:512, 128:256] + r[256:512, 0:128] + r[0:256, 128:256]) + r[0:256, 0:128]
    sig = jax.nn.sigmoid(pre)
    gp = ca[...].reshape(256, 128) * (sig * (1.0 + pre * (1.0 - sig)))
    ghi, glo = split(gp)
    r = mm(wn[...], jnp.concatenate([ghi, glo], axis=1), NN)
    part = (r[512:1024, 128:256] + r[512:1024, 0:128] + r[0:512, 128:256]) + r[0:512, 0:128]
    pv[...] = part.reshape(8, 2, 32, 128)
    xc = send(pv.at[:, oc], px, cdev, sp, rp)
    oo[...] = (pre * sig).reshape(8, 32, 128)
    g2 = jnp.concatenate(
        [jnp.concatenate([ghi, ghi], axis=1), jnp.concatenate([glo, glo], axis=1)], axis=0
    )
    r = mm(g2, mhl, NT)
    gwp[...] = (r[0:256] + r[256:512]).reshape(8, 32, 512)
    xc.wait_recv()
    gz = []
    gs[...] = pv[:, c] + px[...]
    for d in FAR:
        gz.append(send(gs.at[at_z(d)], gv.at[z], zdev(d), sg.at[d], rg.at[d]))
    gv[z] = gs[z]
    oz = [send(oo.at[at_z(d)], orv.at[z], zdev(d), so.at[d], ro.at[d]) for d in FAR]
    wz2 = [send(gwp.at[at_z(d)], gwr.at[z], zdev(d), sgw.at[d], rgw.at[d]) for d in FAR]
    orv[z] = oo[z]
    gwr[z] = gwp[z]

    arrivals = {d: cp for d, cp in zip(FAR, gz)}
    for d in (0, 1, 7, 2, 6, 3, 5, 4):
        if d:
            arrivals[d].wait_recv()
        b = at_z(8 - d)
        ghi, glo = split(gv[b])
        lhs = jnp.concatenate(
            [jnp.concatenate([ghi, ghi], axis=1), jnp.concatenate([glo, glo], axis=1)], axis=0
        )
        for kp in range(4):
            r = mm(lhs, tb[b, kp], NN)
            r = r[0:32] + r[32:64]
            cv[b * 8 + 2 * kp] = r[:, 0:128]
            cv[b * 8 + 2 * kp + 1] = r[:, 128:256]

    q0, q1 = [], []
    for d in (2, 1, 3, 0):
        yd = at_y(d)
        for xo in range(4):
            for r in range(4):
                s = tabs[1, (xo * 4 + yd) * 4 + r]
                piece = cv[s, 0:16]
                if d:
                    sb[0, d, xo, r] = piece
                else:
                    qv[0, y, xo, r] = piece
        if d:
            q0.append(send(sb.at[0, d], qv.at[0, y], ydev(d), sq.at[0, d], rq.at[0, d]))
    for d in (2, 1, 3, 0):
        xd = at_x(d)
        for yo in range(4):
            for r in range(4):
                s = tabs[1, (xd * 4 + yo) * 4 + r]
                piece = cv[s, 16:32]
                if d:
                    sb[1, d, yo, r] = piece
                else:
                    qv[1, x, yo, r] = piece
        if d:
            q1.append(send(sb.at[1, d], qv.at[1, x], xdev(d), sq.at[1, d], rq.at[1, d]))

    for cp in q0:
        cp.wait_recv()
    e0, e1 = [], []
    for d in (2, 1, 3, 0):
        xd = at_x(d)
        total = [jnp.zeros((16, 128), F32) for _ in range(8)]
        for src in range(4):
            for r in range(4):
                w = tabrs[0, src, 2, (xd * 4 + y) * 4 + r]
                piece = qv[0, src, xd, r]
                for i in range(8):
                    total[i] = total[i] + jnp.where(w == i, 1.0, 0.0).astype(F32) * piece
        for i in range(8):
            if d:
                dv[0, d, i] = total[i]
            else:
                ev[0, x, i] = total[i]
        if d:
            e0.append(send(dv.at[0, d], ev.at[0, x], xdev(d), se.at[0, d], re.at[0, d]))
    for cp in q1:
        cp.wait_recv()
    for d in (2, 1, 3, 0):
        yd = at_y(d)
        total = [jnp.zeros((16, 128), F32) for _ in range(8)]
        for src in range(4):
            for r in range(4):
                w = tabrs[1, src, 2, (x * 4 + yd) * 4 + r]
                piece = qv[1, src, yd, r]
                for i in range(8):
                    total[i] = total[i] + jnp.where(w == i, 1.0, 0.0).astype(F32) * piece
        for i in range(8):
            if d:
                dv[1, d, i] = total[i]
            else:
                ev[1, y, i] = total[i]
        if d:
            e1.append(send(dv.at[1, d], ev.at[1, y], ydev(d), se.at[1, d], re.at[1, d]))

    for cp in wz2:
        cp.wait_recv()
    total = gwr[0]
    for q in range(1, 8):
        total = total + gwr[q]
    gw0[0] = total[0:16]
    gw0[1] = total[16:32]
    ga = [send(gw0.at[0], gwa.at[0, x], xdev(d), sga.at[0, d], rga.at[0, d]) for d in (2, 1, 3)]
    ga += [send(gw0.at[1], gwa.at[1, y], ydev(d), sga.at[1, d], rga.at[1, d]) for d in (2, 1, 3)]
    gwa[0, x] = total[0:16]
    gwa[1, y] = total[16:32]
    for cp in oz:
        cp.wait_recv()
    for b in range(8):
        out[:, 128 * b : 128 * b + 128] = orv[b]
    for cp in ga:
        cp.wait_recv()
    for h in range(2):
        half = (gwa[h, 0] + gwa[h, 1]) + (gwa[h, 2] + gwa[h, 3])
        gw1[h] = half
    gb = [send(gw1.at[0], gwb.at[0, y], ydev(d), sgb.at[0, d], rgb.at[0, d]) for d in (2, 1, 3)]
    gb += [send(gw1.at[1], gwb.at[1, x], xdev(d), sgb.at[1, d], rgb.at[1, d]) for d in (2, 1, 3)]
    gwb[0, y] = gw1[0]
    gwb[1, x] = gw1[1]
    for cp in e0 + e1:
        cp.wait_recv()
    for h in range(2):
        for w in range(8):
            gf[16 * h : 16 * h + 16, 128 * w : 128 * w + 128] = (ev[h, 0, w] + ev[h, 1, w]) + (
                ev[h, 2, w] + ev[h, 3, w]
            )
    for cp in gb:
        cp.wait_recv()
    for h in range(2):
        gwt[16 * h : 16 * h + 16] = (gwb[h, 0] + gwb[h, 1]) + (gwb[h, 2] + gwb[h, 3])
    for cp in pending:
        cp.wait_send()


def on_device(feats_t, weight, cot_t, tiles, col_ids, counts):
    vmem = pl.BlockSpec(memory_space=pltpu.VMEM)
    hbm = pl.BlockSpec(memory_space=pltpu.HBM)

    def v(*shape):
        return pltpu.VMEM(shape, F32)

    def dma(*shape):
        return pltpu.SemaphoreType.DMA(shape)

    scratch = [
        v(8, 8, 128, 128),
        pltpu.VMEM((8, 4, 256, 256), BF16),
        v(8, 32, 128),
        v(4, 8, 16, 128),
        v(4, 8, 16, 128),
        v(2, 4, 4, 4, 16, 128),
        v(4, 4, 4, 32, 128),
        v(8, 32, 128),
        v(8, 2, 32, 128),
        v(8, 32, 512),
        pltpu.VMEM((512, 512), BF16),
        pltpu.VMEM((1024, 256), BF16),
        v(8, 32, 128),
        v(8, 32, 128),
        v(8, 32, 128),
        v(8, 2, 32, 128),
        v(8, 32, 128),
        v(8, 32, 128),
        v(8, 32, 128),
        v(8, 32, 512),
        v(8, 32, 512),
        v(2, 16, 512),
        v(2, 4, 16, 512),
        v(2, 16, 512),
        v(2, 4, 16, 512),
        v(64, 32, 128),
        v(2, 4, 4, 4, 16, 128),
        v(2, 4, 4, 4, 16, 128),
        v(2, 4, 8, 16, 128),
        v(2, 4, 8, 16, 128),
        pltpu.VMEM((8, 128), I32),
        pltpu.VMEM((2, 4, 8, 128), I32),
        pltpu.SMEM((8, 128), I32),
        pltpu.SMEM((2, 4, 8, 128), I32),
        pltpu.SMEM((8, 8), I32),
        pltpu.SMEM((8,), I32),
        dma(8), dma(2), dma(12),
        dma(2, 4), dma(2, 4), dma(2, 4), dma(2, 4), dma(2, 4), dma(2, 4),
        dma(8), dma(8), dma(8), dma(8), dma(8), dma(8), dma(8), dma(8),
        pltpu.SemaphoreType.DMA, pltpu.SemaphoreType.DMA,
        dma(8), dma(8), dma(8), dma(8), dma(8), dma(8),
        dma(2, 4), dma(2, 4), dma(2, 4), dma(2, 4),
        dma(2, 4), dma(2, 4), dma(2, 4), dma(2, 4),
    ]
    out, gf, gwt = pl.pallas_call(
        kernel,
        out_shape=(
            jax.ShapeDtypeStruct((32, 1024), F32),
            jax.ShapeDtypeStruct((32, 1024), F32),
            jax.ShapeDtypeStruct((32, 512), F32),
        ),
        in_specs=[hbm] * 6,
        out_specs=(vmem, vmem, vmem),
        scratch_shapes=scratch,
        name="graph_layer",
        cost_estimate=pl.CostEstimate(flops=10**9, bytes_accessed=6 * 10**6, transcendentals=32768),
        compiler_params=pltpu.CompilerParams(
            collective_id=0, has_side_effects=True, vmem_limit_bytes=61936 * 1024
        ),
    )(feats_t, weight.T, cot_t, tiles, col_ids, counts)
    return out, gf, gwt.T


def solution(mesh):
    return jax.shard_map(
        on_device,
        mesh=mesh,
        in_specs=(
            P("feat", "node"),
            P(None, "feat"),
            P("feat", "node"),
            P("node", None, None, None),
            P("node", None),
            P("node"),
        ),
        out_specs=(P("feat", "node"), P("feat", "node"), P(None, "feat")),
        check_vma=False,
    )
```

time: 1880 us -> 69.3 us (0.04)
  waiting for transfers between devices: 1790 us -> 0 us
  Pallas kernels: 0 us -> 63.9 us
  local copies, waits for them, and re-layouts: 34.7 us -> 4.61 us
  matrix products: 19.9 us -> 0 us
    psum x17 -> x0, waiting for transfers between devices: 1610 us -> none  [the longest x16 1530 us: from_root(): return lax.psum(kept, axis)]
    reduce_scatter x1 -> x0, waiting for transfers between devices: 83.4 us -> none  [on_device(): lax.psum_scatter(partial_grad, 'node', scatter_dimension=1, tiled=True)]
    pallas_call x0 -> x1, Pallas kernels: none -> 63.9 us  [on_device(): pl.pallas_call(kernel, out_shape=(jax.ShapeDtypeStruct((32, 1024), F32),...]
    unnamed x5 -> x0, waiting for transfers between devices: 53.5 us -> none
    all_gather x1 -> x0, waiting for transfers between devices: 39.5 us -> none  [on_device(): mixed_full = lax.all_gather(mixed_t, 'feat', axis=0, tiled=True)]
    gather x16 -> x0, local copies, waits for them, and re-layouts: 24.3 us -> none  [section(): picked = jnp.take(shaped, within, axis=1)]
    dot_general x6 -> x0, matrix products: 19.9 us -> none  [the longest x1 6.09 us: on_device(): jnp.einsum('fbkc,bkrc->fbr', selected, tiles, precision=HIGH)]
  transfers between devices with their start and end apart: 20 -> 0, of which waited for: 20 -> 0; matrix products, arithmetic and copies ran while one was open for 1% -> 0% of each run, Pallas kernels for 0% -> 0%
where the time goes in v1:
time: 69.3 us; the launch traced here: 69.2 us
  Pallas kernels  63.9 us (92%)
  local copies, waits for them, and re-layouts  4.61 us (7%)
    pallas_call x1, Pallas kernels, on_device(): pl.pallas_call(kernel, out_shape=(jax.ShapeDtypeStruct((32, 1024), F32),...  63.9 us
    unnamed x3, local copies, waits for them, and re-layouts  4.61 us

profile of v1, /device:TPU:2, one launch (start us, length us, event | category | flops | bytes accessed | tf_op | source)
XLA Modules:
  0.0 69.2 jit_solution(12559677852019731024)
XLA Ops:
  0.6 63.9 %graph_layer.1 = (f32[32,1024]{1,0:T(8,128)}, f32[32,1024]{1,0:T(8,128)}, f32[32,512]{1,0:T(8,128)}) custom-call(f32[32,1024]{1,0:T(8,128)} %feats.1, f32[32,512]{1,0:T(8,128)} %bitcast.2, f32[32,1024]{1,0:T(8,128)} %cot.1, f32[8,8,128,128]{3,2,1,0:T(8,128)} %tiles.1, s32[8,8]{1,0:T(8,128)} %cols_h.1, s32[8]{0:T(128)} %counts_h.1), custom_call_target="tpu_custom_call" | custom-call | flops 1000000000 | bytes 6000000 | tf_op jit(solution)/shard_map/graph_layer/pallas_call | solution.py:450
  64.5 1.6 %copy.12 = f32[32,1024]{1,0:T(8,128)} copy(f32[32,1024]{1,0:T(8,128)} %get-tuple-element.12) | data formatting | bytes 262144
  66.1 1.6 %copy.13 = f32[32,1024]{1,0:T(8,128)} copy(f32[32,1024]{1,0:T(8,128)} %get-tuple-element.13) | data formatting | bytes 262144
  67.7 1.5 %copy.14 = f32[512,32]{0,1:T(8,128)} copy(f32[512,32]{0,1:T(8,128)} %bitcast.3) | data formatting | bytes 131072

commit v2 on v1

--- a/solution.py
+++ b/solution.py
@@ -27,11 +27,11 @@
     feats, wt, cot, tiles, cols_h, counts_h,
     out, gf, gwt,
     t32, tb, f3, av0, av1, sv, rv, mx, mv, wa, wst, wn, ca,
-    oo, orv, pv, px, gs, gv, gwp, gwr, gw0, gwa, gw1, gwb,
+    oo, orv, pv, px, gs, gv, wp0, wp1, ga0, ga1, gbs, gbr, gcs, gcr, ger,
     cv, sb, qv, dv, ev, tab, tabr, tabs, tabrs, cols, counts,
     sem_t, sem_s, sem_i,
     s1, r1, s1t, r1t, s2, r2, sw, rw, sc, rc, sm, rm, sf, rf, sp, rp,
-    so, ro, sg, rg, sgw, rgw, sq, rq, se, re, sga, rga, sgb, rgb,
+    so, ro, sg, rg, sgw, rgw, sq, rq, se, re, sga, rga, sgb, rgb, sge, rge,
 ):
     node = lax.axis_index("node")
     feat = lax.axis_index("feat")
@@ -90,6 +90,17 @@
     peers += [zdev(d) for d in range(1, 8)] + [cdev]
     for p in peers:
         pl.semaphore_signal(barrier, 1, device_id=p, device_id_type=MESH)
+
+    for cp in fcopies:
+        cp.wait()
+    av0[x] = f3[:, 0:16]
+    av1[y] = f3[:, 16:32]
+    pl.semaphore_wait(barrier, len(peers))
+
+    fx = [send(f3.at[:, pl.ds(0, 16)], av0.at[x], xdev(d), s1.at[0, d], r1.at[0, d]) for d in (2, 1, 3)]
+    fy = [send(f3.at[:, pl.ds(16, 16)], av1.at[y], ydev(d), s1.at[1, d], r1.at[1, d]) for d in (2, 1, 3)]
+    cz = [send(cot.at[:, pl.ds(pl.multiple_of(at_z(d) * 128, 128), 128)], ca.at[z], zdev(d), sc.at[d], rc.at[d]) for d in FAR]
+    wz = [send(wt, wa.at[z], zdev(d), sw.at[d], rw.at[d]) for d in FAR]
 
     for cp in ids:
         cp.wait()
@@ -125,32 +136,10 @@
     tabr[0, y] = table
     tabr[1, x] = table
 
-    for cp in fcopies:
-        cp.wait()
-    av0[x] = f3[:, 0:16]
-    av1[y] = f3[:, 16:32]
-    pl.semaphore_wait(barrier, len(peers))
-
     tx = [send(tab, tabr.at[1, x], xdev(d), s1t.at[0, d], r1t.at[0, d]) for d in (1, 2, 3)]
     ty = [send(tab, tabr.at[0, y], ydev(d), s1t.at[1, d], r1t.at[1, d]) for d in (1, 2, 3)]
-    fx = [send(f3.at[:, pl.ds(0, 16)], av0.at[x], xdev(d), s1.at[0, d], r1.at[0, d]) for d in (2, 1, 3)]
-    fy = [send(f3.at[:, pl.ds(16, 16)], av1.at[y], ydev(d), s1.at[1, d], r1.at[1, d]) for d in (2, 1, 3)]
-    cz = [send(cot.at[:, pl.ds(pl.multiple_of(at_z(d) * 128, 128), 128)], ca.at[z], zdev(d), sc.at[d], rc.at[d]) for d in FAR]
-    wz = [send(wt, wa.at[z], zdev(d), sw.at[d], rw.at[d]) for d in FAR]
     to_s = pltpu.make_async_copy(tab, tabs, sem_s.at[0])
     to_s.start()
-
-    def convert(b, carry):
-        pltpu.make_async_copy(tiles.at[b], t32.at[b], sem_t.at[b]).wait()
-        for k in range(8):
-            live = jnp.where(k < counts[b], 1.0, 0.0).astype(F32)
-            hi, lo = split(t32[b, k] * live)
-            q = 128 * (k % 2)
-            tb[b, k // 2, 0:128, q : q + 128] = hi
-            tb[b, k // 2, 128:256, q : q + 128] = lo
-        return carry
-
-    lax.fori_loop(0, 8, convert, 0)
 
     to_s.wait()
     for cp in tx + ty:
@@ -193,19 +182,17 @@
                 send(sv.at[1, d], rv.at[x, :, :, pl.ds(16, 16)], xdev(d), s2.at[1, d], r2.at[1, d])
             )
 
-    for cp in wz:
-        cp.wait_recv()
-    for cp in own:
-        cp.wait()
-    for q in range(8):
-        hi, lo = split(wa[q])
-        wst[32 * q : 32 * q + 32] = hi
-        wst[256 + 32 * q : 288 + 32 * q] = lo
-    for g in range(4):
-        turned = jnp.transpose(wa[:, :, 128 * g : 128 * g + 128].reshape(256, 128))
-        hi, lo = split(turned)
-        wn[128 * g : 128 * g + 128] = hi
-        wn[512 + 128 * g : 640 + 128 * g] = lo
+    def convert(b, carry):
+        pltpu.make_async_copy(tiles.at[b], t32.at[b], sem_t.at[b]).wait()
+        for k in range(8):
+            live = jnp.where(k < counts[b], 1.0, 0.0).astype(F32)
+            hi, lo = split(t32[b, k] * live)
+            q = 128 * (k % 2)
+            tb[b, k // 2, 0:128, q : q + 128] = hi
+            tb[b, k // 2, 128:256, q : q + 128] = lo
+        return carry
+
+    lax.fori_loop(0, 8, convert, 0)
 
     for cp in leg2:
         cp.wait_recv()
@@ -236,6 +223,20 @@
             mz.append(send(mx.at[d], mv.at[z, c], zdev(d), sm.at[d], rm.at[d]))
         else:
             mv[z, c] = mixed
+    for cp in wz:
+        cp.wait_recv()
+    for cp in own:
+        cp.wait()
+    for q in range(8):
+        hi, lo = split(wa[q])
+        wst[32 * q : 32 * q + 32] = hi
+        wst[256 + 32 * q : 288 + 32 * q] = lo
+    for g in range(4):
+        turned = jnp.transpose(wa[:, :, 128 * g : 128 * g + 128].reshape(256, 128))
+        hi, lo = split(turned)
+        wn[128 * g : 128 * g + 128] = hi
+        wn[512 + 128 * g : 640 + 128 * g] = lo
+
     fz = [send(mv.at[z, c], mv.at[z, c], cdev, sf.at[0], rf.at[0])]
     for i, d in enumerate(FAR):
         mz[i].wait_recv()
@@ -262,17 +263,27 @@
         [jnp.concatenate([ghi, ghi], axis=1), jnp.concatenate([glo, glo], axis=1)], axis=0
     )
     r = mm(g2, mhl, NT)
-    gwp[...] = (r[0:256] + r[256:512]).reshape(8, 32, 512)
+    r = r[0:256] + r[256:512]
+    for q in range(8):
+        for a in range(4):
+            for g in range(4):
+                chunk = r[32 * q + 8 * a : 32 * q + 8 * a + 8, 128 * g : 128 * g + 128]
+                if q < 4:
+                    wp0[a, g, q] = chunk
+                else:
+                    wp1[g, a, q - 4] = chunk
     xc.wait_recv()
     gz = []
     gs[...] = pv[:, c] + px[...]
     for d in FAR:
         gz.append(send(gs.at[at_z(d)], gv.at[z], zdev(d), sg.at[d], rg.at[d]))
     gv[z] = gs[z]
+    ga = [send(wp0.at[at_x(d)], ga0.at[x], xdev(d), sga.at[0, d], rga.at[0, d]) for d in (2, 1, 3)]
+    ga += [send(wp1.at[at_y(d)], ga1.at[y], ydev(d), sga.at[1, d], rga.at[1, d]) for d in (2, 1, 3)]
+    ga0[x] = wp0[x]
+    ga1[y] = wp1[y]
     oz = [send(oo.at[at_z(d)], orv.at[z], zdev(d), so.at[d], ro.at[d]) for d in FAR]
-    wz2 = [send(gwp.at[at_z(d)], gwr.at[z], zdev(d), sgw.at[d], rgw.at[d]) for d in FAR]
     orv[z] = oo[z]
-    gwr[z] = gwp[z]
 
     arrivals = {d: cp for d, cp in zip(FAR, gz)}
     for d in (0, 1, 7, 2, 6, 3, 5, 4):
@@ -289,6 +300,15 @@
             cv[b * 8 + 2 * kp] = r[:, 0:128]
             cv[b * 8 + 2 * kp + 1] = r[:, 128:256]
 
+    for cp in ga:
+        cp.wait_recv()
+    gbs[0] = (ga0[0] + ga0[1]) + (ga0[2] + ga0[3])
+    gbs[1] = (ga1[0] + ga1[1]) + (ga1[2] + ga1[3])
+    gb = [send(gbs.at[0, at_y(d)], gbr.at[0, y], ydev(d), sgb.at[0, d], rgb.at[0, d]) for d in (2, 1, 3)]
+    gb += [send(gbs.at[1, at_x(d)], gbr.at[1, x], xdev(d), sgb.at[1, d], rgb.at[1, d]) for d in (2, 1, 3)]
+    gbr[0, y] = gbs[0, y]
+    gbr[1, x] = gbs[1, x]
+
     q0, q1 = [], []
     for d in (2, 1, 3, 0):
         yd = at_y(d)
@@ -314,6 +334,20 @@
                     qv[1, x, yo, r] = piece
         if d:
             q1.append(send(sb.at[1, d], qv.at[1, x], xdev(d), sq.at[1, d], rq.at[1, d]))
+
+    for cp in gb:
+        cp.wait_recv()
+    for h in range(2):
+        gcs[4 * h : 4 * h + 4] = (gbr[h, 0] + gbr[h, 1]) + (gbr[h, 2] + gbr[h, 3])
+    gc = [send(gcs.at[at_z(d)], gcr.at[z], zdev(d), sgw.at[d], rgw.at[d]) for d in FAR]
+    gcr[z] = gcs[z]
+    for cp in gc:
+        cp.wait_recv()
+    total = gcr[0]
+    for q in range(1, 8):
+        total = total + gcr[q]
+    ger[x, y] = total
+    gy = [send(ger.at[x, y], ger.at[x, y], ydev(d), sge.at[0, d], rge.at[0, d]) for d in (2, 1, 3)]
 
     for cp in q0:
         cp.wait_recv()
@@ -353,30 +387,13 @@
         if d:
             e1.append(send(dv.at[1, d], ev.at[1, y], ydev(d), se.at[1, d], re.at[1, d]))
 
-    for cp in wz2:
-        cp.wait_recv()
-    total = gwr[0]
-    for q in range(1, 8):
-        total = total + gwr[q]
-    gw0[0] = total[0:16]
-    gw0[1] = total[16:32]
-    ga = [send(gw0.at[0], gwa.at[0, x], xdev(d), sga.at[0, d], rga.at[0, d]) for d in (2, 1, 3)]
-    ga += [send(gw0.at[1], gwa.at[1, y], ydev(d), sga.at[1, d], rga.at[1, d]) for d in (2, 1, 3)]
-    gwa[0, x] = total[0:16]
-    gwa[1, y] = total[16:32]
+    for cp in gy:
+        cp.wait_recv()
+    gx = [send(ger.at[x], ger.at[x], xdev(d), sge.at[1, d], rge.at[1, d]) for d in (2, 1, 3)]
     for cp in oz:
         cp.wait_recv()
     for b in range(8):
         out[:, 128 * b : 128 * b + 128] = orv[b]
-    for cp in ga:
-        cp.wait_recv()
-    for h in range(2):
-        half = (gwa[h, 0] + gwa[h, 1]) + (gwa[h, 2] + gwa[h, 3])
-        gw1[h] = half
-    gb = [send(gw1.at[0], gwb.at[0, y], ydev(d), sgb.at[0, d], rgb.at[0, d]) for d in (2, 1, 3)]
-    gb += [send(gw1.at[1], gwb.at[1, x], xdev(d), sgb.at[1, d], rgb.at[1, d]) for d in (2, 1, 3)]
-    gwb[0, y] = gw1[0]
-    gwb[1, x] = gw1[1]
     for cp in e0 + e1:
         cp.wait_recv()
     for h in range(2):
@@ -384,12 +401,26 @@
             gf[16 * h : 16 * h + 16, 128 * w : 128 * w + 128] = (ev[h, 0, w] + ev[h, 1, w]) + (
                 ev[h, 2, w] + ev[h, 3, w]
             )
-    for cp in gb:
-        cp.wait_recv()
-    for h in range(2):
-        gwt[16 * h : 16 * h + 16] = (gwb[h, 0] + gwb[h, 1]) + (gwb[h, 2] + gwb[h, 3])
+    for cp in gx:
+        cp.wait_recv()
+    for a in range(4):
+        for g in range(4):
+            gwt[8 * a : 8 * a + 8, 128 * g : 128 * g + 128] = ger[a, g]
     for cp in pending:
         cp.wait_send()
+
+
+def hand_over(a, b, c, out, gf, gwt, va, vb, vc, sem):
+    trips = ((a, va, out), (b, vb, gf), (c, vc, gwt))
+    inward = [pltpu.make_async_copy(src, via, sem.at[0, i]) for i, (src, via, _) in enumerate(trips)]
+    outward = [pltpu.make_async_copy(via, dst, sem.at[1, i]) for i, (_, via, dst) in enumerate(trips)]
+    for cp in inward:
+        cp.start()
+    for first, second in zip(inward, outward):
+        first.wait()
+        second.start()
+    for cp in outward:
+        cp.wait()
 
 
 def on_device(feats_t, weight, cot_t, tiles, col_ids, counts):
@@ -422,12 +453,15 @@
         v(8, 32, 128),
         v(8, 32, 128),
         v(8, 32, 128),
-        v(8, 32, 512),
-        v(8, 32, 512),
-        v(2, 16, 512),
-        v(2, 4, 16, 512),
-        v(2, 16, 512),
-        v(2, 4, 16, 512),
+        v(4, 4, 4, 8, 128),
+        v(4, 4, 4, 8, 128),
+        v(4, 4, 4, 8, 128),
+        v(4, 4, 4, 8, 128),
+        v(2, 4, 4, 8, 128),
+        v(2, 4, 4, 8, 128),
+        v(8, 8, 128),
+        v(8, 8, 128),
+        v(4, 4, 8, 128),
         v(64, 32, 128),
         v(2, 4, 4, 4, 16, 128),
         v(2, 4, 4, 4, 16, 128),
@@ -445,7 +479,7 @@
         pltpu.SemaphoreType.DMA, pltpu.SemaphoreType.DMA,
         dma(8), dma(8), dma(8), dma(8), dma(8), dma(8),
         dma(2, 4), dma(2, 4), dma(2, 4), dma(2, 4),
-        dma(2, 4), dma(2, 4), dma(2, 4), dma(2, 4),
+        dma(2, 4), dma(2, 4), dma(2, 4), dma(2, 4), dma(2, 4), dma(2, 4),
     ]
     out, gf, gwt = pl.pallas_call(
         kernel,
@@ -463,6 +497,20 @@
             collective_id=0, has_side_effects=True, vmem_limit_bytes=61936 * 1024
         ),
     )(feats_t, weight.T, cot_t, tiles, col_ids, counts)
+    anywhere = pl.BlockSpec(memory_space=pl.ANY)
+    out, gf, gwt = pl.pallas_call(
+        hand_over,
+        out_shape=(
+            jax.ShapeDtypeStruct((32, 1024), F32),
+            jax.ShapeDtypeStruct((32, 1024), F32),
+            jax.ShapeDtypeStruct((32, 512), F32),
+        ),
+        in_specs=[anywhere] * 3,
+        out_specs=(anywhere,) * 3,
+        scratch_shapes=[v(32, 1024), v(32, 1024), v(32, 512), dma(2, 3)],
+        name="hand_over",
+        cost_estimate=pl.CostEstimate(flops=0, bytes_accessed=2 * 320 * 1024, transcendentals=0),
+    )(out, gf, gwt)
     return out, gf, gwt.T
 
 

time: 69.3 us -> 61.2 us (0.88)
  local copies, waits for them, and re-layouts: 4.61 us -> 0 us
  Pallas kernels: 63.9 us -> 60.5 us
    pallas_call x1, Pallas kernels: 63.9 us -> 58.8 us  [on_device(): pl.pallas_call(kernel, out_shape=(jax.ShapeDtypeStruct((32, 1024), F32),...]
    unnamed x3 -> x0, local copies, waits for them, and re-layouts: 4.61 us -> none
    pallas_call x0 -> x1, Pallas kernels: none -> 1.69 us  [on_device(): pl.pallas_call(hand_over, out_shape=(jax.ShapeDtypeStruct((32, 1024), F32...]
where the time goes in v2:
time: 61.2 us; the launch traced here: 61.1 us
  Pallas kernels  60.5 us (99%)
  between operations  0.64 us (1%)
    pallas_call x1, Pallas kernels, on_device(): pl.pallas_call(kernel, out_shape=(jax.ShapeDtypeStruct((32, 1024), F32),...  58.8 us
    pallas_call x1, Pallas kernels, on_device(): pl.pallas_call(hand_over, out_shape=(jax.ShapeDtypeStruct((32, 1024), F32...  1.69 us

profile of v2, /device:TPU:2, one launch (start us, length us, event | category | flops | bytes accessed | tf_op | source)
XLA Modules:
  0.0 61.1 jit_solution(1297219451891196932)
XLA Ops:
  0.6 58.8 %graph_layer.1 = (f32[32,1024]{1,0:T(8,128)}, f32[32,1024]{1,0:T(8,128)}, f32[32,512]{1,0:T(8,128)}) custom-call(f32[32,1024]{1,0:T(8,128)} %feats.1, f32[32,512]{1,0:T(8,128)} %bitcast.2, f32[32,1024]{1,0:T(8,128)} %cot.1, f32[8,8,128,128]{3,2,1,0:T(8,128)} %tiles.1, s32[8,8]{1,0:T(8,128)} %cols_h.1, s32[8]{0:T(128)} %counts_h.1), custom_call_target="tpu_custom_call" | custom-call | flops 1000000000 | bytes 6000000 | tf_op jit(solution)/shard_map/graph_layer/pallas_call | solution.py:484
  59.4 1.7 %hand_over.1 = (f32[32,1024]{1,0:T(8,128)}, f32[32,1024]{1,0:T(8,128)}, f32[32,512]{1,0:T(8,128)}) custom-call(f32[32,1024]{1,0:T(8,128)} %get-tuple-element.9.a, f32[32,1024]{1,0:T(8,128)} %get-tuple-element.10.b, f32[32,512]{1,0:T(8,128)} %get-tuple-element.11.c), custom_call_target="tpu_custom_call" | custom-call | bytes 655360 | tf_op jit(solution)/shard_map/hand_over/pallas_call | solution.py:501

commit v3 on v2

--- a/solution.py
+++ b/solution.py
@@ -12,6 +12,7 @@
 NN = (((1,), (0,)), ((), ()))
 NT = (((1,), (1,)), ((), ()))
 FAR = (4, 3, 5, 2, 6, 1, 7)
+PLANE = sorted(((i, j) for i in range(4) for j in range(4) if i + j), key=lambda d: -min(d[0], 4 - d[0]) - min(d[1], 4 - d[1]))
 
 
 def split(v):
@@ -26,12 +27,12 @@
 def kernel(
     feats, wt, cot, tiles, cols_h, counts_h,
     out, gf, gwt,
-    t32, tb, f3, av0, av1, sv, rv, mx, mv, wa, wst, wn, ca,
-    oo, orv, pv, px, gs, gv, wp0, wp1, ga0, ga1, gbs, gbr, gcs, gcr, ger,
+    t32, tb, fo, a01, a02, a03, a11, a12, a13, sv, rv, mx, mv, wa, wst, wn, ca,
+    oo, orv, pv, px, gs, gv, wp, gar, gcs, gcr, ger,
     cv, sb, qv, dv, ev, tab, tabr, tabs, tabrs, cols, counts,
     sem_t, sem_s, sem_i,
     s1, r1, s1t, r1t, s2, r2, sw, rw, sc, rc, sm, rm, sf, rf, sp, rp,
-    so, ro, sg, rg, sgw, rgw, sq, rq, se, re, sga, rga, sgb, rgb, sge, rge,
+    so, ro, sg, rg, sgw, rgw, sq, rq, se, re, sga, rga, sge, rge,
 ):
     node = lax.axis_index("node")
     feat = lax.axis_index("feat")
@@ -53,6 +54,9 @@
 
     def ydev(d):
         return (x * 4 + at_y(d), feat)
+
+    def xydev(dx, dy):
+        return (at_x(dx) * 4 + at_y(dy), feat)
 
     def zdev(d):
         return (node, at_z(d) * 2 + c)
@@ -74,33 +78,31 @@
         pltpu.make_async_copy(counts_h, counts, sem_i.at[1]),
     ]
     fcopies = [
-        pltpu.make_async_copy(feats.at[:, pl.ds(128 * w, 128)], f3.at[w], sem_i.at[2 + w])
+        pltpu.make_async_copy(feats.at[:, pl.ds(128 * w, 128)], fo.at[w], sem_i.at[2 + w])
         for w in range(8)
     ]
     own = [
         pltpu.make_async_copy(wt, wa.at[z], sem_i.at[10]),
         pltpu.make_async_copy(cot.at[:, pl.ds(pl.multiple_of(z * 128, 128), 128)], ca.at[z], sem_i.at[11]),
     ]
-    for cp in ids + fcopies + own:
+    for cp in fcopies + ids + own:
         cp.start()
     for b in range(8):
         pltpu.make_async_copy(tiles.at[b], t32.at[b], sem_t.at[b]).start()
     barrier = pltpu.get_barrier_semaphore()
-    peers = [xdev(d) for d in (1, 2, 3)] + [ydev(d) for d in (1, 2, 3)]
-    peers += [zdev(d) for d in range(1, 8)] + [cdev]
+    peers = [zdev(d) for d in (4, 3, 5, 2, 6, 1, 7)] + [xydev(*d) for d in PLANE] + [cdev]
     for p in peers:
         pl.semaphore_signal(barrier, 1, device_id=p, device_id_type=MESH)
 
     for cp in fcopies:
         cp.wait()
-    av0[x] = f3[:, 0:16]
-    av1[y] = f3[:, 16:32]
     pl.semaphore_wait(barrier, len(peers))
 
-    fx = [send(f3.at[:, pl.ds(0, 16)], av0.at[x], xdev(d), s1.at[0, d], r1.at[0, d]) for d in (2, 1, 3)]
-    fy = [send(f3.at[:, pl.ds(16, 16)], av1.at[y], ydev(d), s1.at[1, d], r1.at[1, d]) for d in (2, 1, 3)]
-    cz = [send(cot.at[:, pl.ds(pl.multiple_of(at_z(d) * 128, 128), 128)], ca.at[z], zdev(d), sc.at[d], rc.at[d]) for d in FAR]
-    wz = [send(wt, wa.at[z], zdev(d), sw.at[d], rw.at[d]) for d in FAR]
+    heard = ((None, a01, a02, a03), (None, a11, a12, a13))
+    fx, fy = {}, {}
+    for d in (1, 3, 2):
+        fx[d] = send(fo.at[:, pl.ds(0, 16)], heard[0][d], xdev(d), s1.at[0, d], r1.at[0, d])
+        fy[d] = send(fo.at[:, pl.ds(16, 16)], heard[1][d], ydev(d), s1.at[1, d], r1.at[1, d])
 
     for cp in ids:
         cp.wait()
@@ -140,7 +142,8 @@
     ty = [send(tab, tabr.at[0, y], ydev(d), s1t.at[1, d], r1t.at[1, d]) for d in (1, 2, 3)]
     to_s = pltpu.make_async_copy(tab, tabs, sem_s.at[0])
     to_s.start()
-
+    cz = [send(cot.at[:, pl.ds(pl.multiple_of(at_z(d) * 128, 128), 128)], ca.at[z], zdev(d), sc.at[d], rc.at[d]) for d in FAR]
+    wz = [send(wt, wa.at[z], zdev(d), sw.at[d], rw.at[d]) for d in FAR]
     to_s.wait()
     for cp in tx + ty:
         cp.wait_recv()
@@ -148,39 +151,31 @@
     to_rs.start()
     to_rs.wait()
 
-    for cp in fx:
-        cp.wait_recv()
     leg2 = []
-    for d in (2, 1, 3, 0):
-        yd = at_y(d)
-        for xo in range(4):
-            for r in range(4):
-                w = tabrs[0, yd, 2, (xo * 4 + y) * 4 + r]
-                block = av0[xo, w]
-                if d:
-                    sv[0, d, xo, r] = block
-                else:
-                    rv[xo, y, r, 0:16] = block
-        if d:
-            leg2.append(
-                send(sv.at[0, d], rv.at[:, y, :, pl.ds(0, 16)], ydev(d), s2.at[0, d], r2.at[0, d])
-            )
-    for cp in fy:
-        cp.wait_recv()
-    for d in (2, 1, 3, 0):
-        xd = at_x(d)
-        for yo in range(4):
-            for r in range(4):
-                w = tabrs[1, xd, 2, (x * 4 + yo) * 4 + r]
-                block = av1[yo, w]
-                if d:
-                    sv[1, d, yo, r] = block
-                else:
-                    rv[x, yo, r, 16:32] = block
-        if d:
-            leg2.append(
-                send(sv.at[1, d], rv.at[x, :, :, pl.ds(16, 16)], xdev(d), s2.at[1, d], r2.at[1, d])
-            )
+    for g in (0, 1, 3, 2):
+        for h in range(2):
+            if g:
+                (fx, fy)[h][g].wait_recv()
+            xo, yo = at_x(4 - g), at_y(4 - g)
+            for d in (2, 1, 3, 0):
+                for r in range(4):
+                    if h == 0:
+                        w = tabrs[0, at_y(d), 2, (xo * 4 + y) * 4 + r]
+                    else:
+                        w = tabrs[1, at_x(d), 2, (x * 4 + yo) * 4 + r]
+                    block = heard[h][g][w] if g else fo[w, 16 * h : 16 * h + 16]
+                    if d:
+                        sv[h, g, d, r] = block
+                    elif h == 0:
+                        rv[xo, y, r, 0:16] = block
+                    else:
+                        rv[x, yo, r, 16:32] = block
+                if d and h == 0:
+                    to = rv.at[xo, y, :, pl.ds(0, 16)]
+                    leg2.append(send(sv.at[0, g, d], to, ydev(d), s2.at[0, g, d], r2.at[0, g, d]))
+                elif d:
+                    to = rv.at[x, yo, :, pl.ds(16, 16)]
+                    leg2.append(send(sv.at[1, g, d], to, xdev(d), s2.at[1, g, d], r2.at[1, g, d]))
 
     def convert(b, carry):
         pltpu.make_async_copy(tiles.at[b], t32.at[b], sem_t.at[b]).wait()
@@ -268,20 +263,18 @@
         for a in range(4):
             for g in range(4):
                 chunk = r[32 * q + 8 * a : 32 * q + 8 * a + 8, 128 * g : 128 * g + 128]
-                if q < 4:
-                    wp0[a, g, q] = chunk
-                else:
-                    wp1[g, a, q - 4] = chunk
+                wp[a, g, q] = chunk
     xc.wait_recv()
     gz = []
     gs[...] = pv[:, c] + px[...]
     for d in FAR:
         gz.append(send(gs.at[at_z(d)], gv.at[z], zdev(d), sg.at[d], rg.at[d]))
     gv[z] = gs[z]
-    ga = [send(wp0.at[at_x(d)], ga0.at[x], xdev(d), sga.at[0, d], rga.at[0, d]) for d in (2, 1, 3)]
-    ga += [send(wp1.at[at_y(d)], ga1.at[y], ydev(d), sga.at[1, d], rga.at[1, d]) for d in (2, 1, 3)]
-    ga0[x] = wp0[x]
-    ga1[y] = wp1[y]
+    ga = [
+        send(wp.at[at_x(i), at_y(j)], gar.at[x, y], xydev(i, j), sga.at[i, j], rga.at[i, j])
+        for i, j in PLANE
+    ]
+    gar[x, y] = wp[x, y]
     oz = [send(oo.at[at_z(d)], orv.at[z], zdev(d), so.at[d], ro.at[d]) for d in FAR]
     orv[z] = oo[z]
 
@@ -300,108 +293,86 @@
             cv[b * 8 + 2 * kp] = r[:, 0:128]
             cv[b * 8 + 2 * kp + 1] = r[:, 128:256]
 
+    back = {}
+    for g in (2, 1, 3, 0):
+        for h in range(2):
+            for d in (2, 1, 3, 0):
+                for r in range(4):
+                    if h == 0:
+                        s = tabs[1, (at_x(g) * 4 + at_y(d)) * 4 + r]
+                    else:
+                        s = tabs[1, (at_x(d) * 4 + at_y(g)) * 4 + r]
+                    piece = cv[s, 16 * h : 16 * h + 16]
+                    if d:
+                        sb[h, g, d, r] = piece
+                    elif h == 0:
+                        qv[0, g, y, r] = piece
+                    else:
+                        qv[1, g, x, r] = piece
+                if d and h == 0:
+                    to = qv.at[0, g, y]
+                    back[h, g, d] = send(sb.at[0, g, d], to, ydev(d), sq.at[0, g, d], rq.at[0, g, d])
+                elif d:
+                    to = qv.at[1, g, x]
+                    back[h, g, d] = send(sb.at[1, g, d], to, xdev(d), sq.at[1, g, d], rq.at[1, g, d])
+
     for cp in ga:
         cp.wait_recv()
-    gbs[0] = (ga0[0] + ga0[1]) + (ga0[2] + ga0[3])
-    gbs[1] = (ga1[0] + ga1[1]) + (ga1[2] + ga1[3])
-    gb = [send(gbs.at[0, at_y(d)], gbr.at[0, y], ydev(d), sgb.at[0, d], rgb.at[0, d]) for d in (2, 1, 3)]
-    gb += [send(gbs.at[1, at_x(d)], gbr.at[1, x], xdev(d), sgb.at[1, d], rgb.at[1, d]) for d in (2, 1, 3)]
-    gbr[0, y] = gbs[0, y]
-    gbr[1, x] = gbs[1, x]
-
-    q0, q1 = [], []
-    for d in (2, 1, 3, 0):
-        yd = at_y(d)
-        for xo in range(4):
-            for r in range(4):
-                s = tabs[1, (xo * 4 + yd) * 4 + r]
-                piece = cv[s, 0:16]
-                if d:
-                    sb[0, d, xo, r] = piece
-                else:
-                    qv[0, y, xo, r] = piece
-        if d:
-            q0.append(send(sb.at[0, d], qv.at[0, y], ydev(d), sq.at[0, d], rq.at[0, d]))
-    for d in (2, 1, 3, 0):
-        xd = at_x(d)
-        for yo in range(4):
-            for r in range(4):
-                s = tabs[1, (xd * 4 + yo) * 4 + r]
-                piece = cv[s, 16:32]
-                if d:
-                    sb[1, d, yo, r] = piece
-                else:
-                    qv[1, x, yo, r] = piece
-        if d:
-            q1.append(send(sb.at[1, d], qv.at[1, x], xdev(d), sq.at[1, d], rq.at[1, d]))
-
-    for cp in gb:
-        cp.wait_recv()
-    for h in range(2):
-        gcs[4 * h : 4 * h + 4] = (gbr[h, 0] + gbr[h, 1]) + (gbr[h, 2] + gbr[h, 3])
+    held = gar[0, 0]
+    for q in range(1, 16):
+        held = held + gar[q // 4, q % 4]
+    gcs[...] = held
     gc = [send(gcs.at[at_z(d)], gcr.at[z], zdev(d), sgw.at[d], rgw.at[d]) for d in FAR]
     gcr[z] = gcs[z]
-    for cp in gc:
-        cp.wait_recv()
-    total = gcr[0]
-    for q in range(1, 8):
-        total = total + gcr[q]
-    ger[x, y] = total
-    gy = [send(ger.at[x, y], ger.at[x, y], ydev(d), sge.at[0, d], rge.at[0, d]) for d in (2, 1, 3)]
-
-    for cp in q0:
-        cp.wait_recv()
-    e0, e1 = [], []
-    for d in (2, 1, 3, 0):
-        xd = at_x(d)
-        total = [jnp.zeros((16, 128), F32) for _ in range(8)]
-        for src in range(4):
-            for r in range(4):
-                w = tabrs[0, src, 2, (xd * 4 + y) * 4 + r]
-                piece = qv[0, src, xd, r]
-                for i in range(8):
-                    total[i] = total[i] + jnp.where(w == i, 1.0, 0.0).astype(F32) * piece
-        for i in range(8):
-            if d:
-                dv[0, d, i] = total[i]
-            else:
-                ev[0, x, i] = total[i]
-        if d:
-            e0.append(send(dv.at[0, d], ev.at[0, x], xdev(d), se.at[0, d], re.at[0, d]))
-    for cp in q1:
-        cp.wait_recv()
-    for d in (2, 1, 3, 0):
-        yd = at_y(d)
-        total = [jnp.zeros((16, 128), F32) for _ in range(8)]
-        for src in range(4):
-            for r in range(4):
-                w = tabrs[1, src, 2, (x * 4 + yd) * 4 + r]
-                piece = qv[1, src, yd, r]
-                for i in range(8):
-                    total[i] = total[i] + jnp.where(w == i, 1.0, 0.0).astype(F32) * piece
-        for i in range(8):
-            if d:
-                dv[1, d, i] = total[i]
-            else:
-                ev[1, y, i] = total[i]
-        if d:
-            e1.append(send(dv.at[1, d], ev.at[1, y], ydev(d), se.at[1, d], re.at[1, d]))
-
-    for cp in gy:
-        cp.wait_recv()
-    gx = [send(ger.at[x], ger.at[x], xdev(d), sge.at[1, d], rge.at[1, d]) for d in (2, 1, 3)]
+
+    last = []
+    for g in (2, 1, 3, 0):
+        for h in range(2):
+            for d in (1, 3, 2):
+                back[h, g, d].wait_recv()
+            total = [jnp.zeros((16, 128), F32) for _ in range(8)]
+            for src in range(4):
+                for r in range(4):
+                    if h == 0:
+                        w = tabrs[0, src, 2, (at_x(g) * 4 + y) * 4 + r]
+                    else:
+                        w = tabrs[1, src, 2, (x * 4 + at_y(g)) * 4 + r]
+                    piece = qv[h, g, src, r]
+                    for i in range(8):
+                        total[i] = total[i] + jnp.where(w == i, 1.0, 0.0).astype(F32) * piece
+            for i in range(8):
+                if g:
+                    dv[h, g, i] = total[i]
+                else:
+                    ev[h, 0, i] = total[i]
+            if g:
+                device = ydev(g) if h else xdev(g)
+                last.append(send(dv.at[h, g], ev.at[h, g], device, se.at[h, g], re.at[h, g]))
+
+        if g == 1:
+            for cp in gc:
+                cp.wait_recv()
+            held = gcr[0]
+            for q in range(1, 8):
+                held = held + gcr[q]
+            ger[x, y] = held
+            ge = [
+                send(ger.at[x, y], ger.at[x, y], xydev(i, j), sge.at[i, j], rge.at[i, j])
+                for i, j in PLANE
+            ]
+
     for cp in oz:
         cp.wait_recv()
     for b in range(8):
         out[:, 128 * b : 128 * b + 128] = orv[b]
-    for cp in e0 + e1:
+    for cp in last:
         cp.wait_recv()
     for h in range(2):
         for w in range(8):
             gf[16 * h : 16 * h + 16, 128 * w : 128 * w + 128] = (ev[h, 0, w] + ev[h, 1, w]) + (
                 ev[h, 2, w] + ev[h, 3, w]
             )
-    for cp in gx:
+    for cp in ge:
         cp.wait_recv()
     for a in range(4):
         for g in range(4):
@@ -437,8 +408,8 @@
         v(8, 8, 128, 128),
         pltpu.VMEM((8, 4, 256, 256), BF16),
         v(8, 32, 128),
-        v(4, 8, 16, 128),
-        v(4, 8, 16, 128),
+        v(8, 16, 128), v(8, 16, 128), v(8, 16, 128),
+        v(8, 16, 128), v(8, 16, 128), v(8, 16, 128),
         v(2, 4, 4, 4, 16, 128),
         v(4, 4, 4, 32, 128),
         v(8, 32, 128),
@@ -453,12 +424,8 @@
         v(8, 32, 128),
         v(8, 32, 128),
         v(8, 32, 128),
-        v(4, 4, 4, 8, 128),
-        v(4, 4, 4, 8, 128),
-        v(4, 4, 4, 8, 128),
-        v(4, 4, 4, 8, 128),
-        v(2, 4, 4, 8, 128),
-        v(2, 4, 4, 8, 128),
+        v(4, 4, 8, 8, 128),
+        v(4, 4, 8, 8, 128),
         v(8, 8, 128),
         v(8, 8, 128),
         v(4, 4, 8, 128),
@@ -474,12 +441,12 @@
         pltpu.SMEM((8, 8), I32),
         pltpu.SMEM((8,), I32),
         dma(8), dma(2), dma(12),
-        dma(2, 4), dma(2, 4), dma(2, 4), dma(2, 4), dma(2, 4), dma(2, 4),
+        dma(2, 4), dma(2, 4), dma(2, 4), dma(2, 4), dma(2, 4, 4), dma(2, 4, 4),
         dma(8), dma(8), dma(8), dma(8), dma(8), dma(8), dma(8), dma(8),
         pltpu.SemaphoreType.DMA, pltpu.SemaphoreType.DMA,
         dma(8), dma(8), dma(8), dma(8), dma(8), dma(8),
-        dma(2, 4), dma(2, 4), dma(2, 4), dma(2, 4),
-        dma(2, 4), dma(2, 4), dma(2, 4), dma(2, 4), dma(2, 4), dma(2, 4),
+        dma(2, 4, 4), dma(2, 4, 4), dma(2, 4), dma(2, 4),
+        dma(4, 4), dma(4, 4), dma(4, 4), dma(4, 4),
     ]
     out, gf, gwt = pl.pallas_call(
         kernel,

time: 61.2 us -> 56.8 us (0.928)
  Pallas kernels: 60.5 us -> 55.8 us
    pallas_call x1, Pallas kernels: 58.8 us -> 54.1 us  [on_device(): pl.pallas_call(kernel, out_shape=(jax.ShapeDtypeStruct((32, 1024), F32),...]
where the time goes in v3:
time: 56.8 us; the launch traced here: 56.5 us
  Pallas kernels  55.8 us (98%)
  between operations  0.64 us (1%)
    pallas_call x1, Pallas kernels, on_device(): pl.pallas_call(kernel, out_shape=(jax.ShapeDtypeStruct((32, 1024), F32),...  54.1 us
    pallas_call x1, Pallas kernels, on_device(): pl.pallas_call(hand_over, out_shape=(jax.ShapeDtypeStruct((32, 1024), F32...  1.69 us

profile of v3, /device:TPU:2, one launch (start us, length us, event | category | flops | bytes accessed | tf_op | source)
XLA Modules:
  0.0 56.5 jit_solution(6022165872606183386)
XLA Ops:
  0.6 54.1 %graph_layer.1 = (f32[32,1024]{1,0:T(8,128)}, f32[32,1024]{1,0:T(8,128)}, f32[32,512]{1,0:T(8,128)}) custom-call(f32[32,1024]{1,0:T(8,128)} %feats.1, f32[32,512]{1,0:T(8,128)} %bitcast.2, f32[32,1024]{1,0:T(8,128)} %cot.1, f32[8,8,128,128]{3,2,1,0:T(8,128)} %tiles.1, s32[8,8]{1,0:T(8,128)} %cols_h.1, s32[8]{0:T(128)} %counts_h.1), custom_call_target="tpu_custom_call" | custom-call | flops 1000000000 | bytes 6000000 | tf_op jit(solution)/shard_map/graph_layer/pallas_call | solution.py:451
  54.8 1.7 %hand_over.1 = (f32[32,1024]{1,0:T(8,128)}, f32[32,1024]{1,0:T(8,128)}, f32[32,512]{1,0:T(8,128)}) custom-call(f32[32,1024]{1,0:T(8,128)} %get-tuple-element.9.a, f32[32,1024]{1,0:T(8,128)} %get-tuple-element.10.b, f32[32,512]{1,0:T(8,128)} %get-tuple-element.11.c), custom_call_target="tpu_custom_call" | custom-call | bytes 655360 | tf_op jit(solution)/shard_map/hand_over/pallas_call | solution.py:468

commit v4 on v3

--- a/solution.py
+++ b/solution.py
@@ -93,16 +93,6 @@
     peers = [zdev(d) for d in (4, 3, 5, 2, 6, 1, 7)] + [xydev(*d) for d in PLANE] + [cdev]
     for p in peers:
         pl.semaphore_signal(barrier, 1, device_id=p, device_id_type=MESH)
-
-    for cp in fcopies:
-        cp.wait()
-    pl.semaphore_wait(barrier, len(peers))
-
-    heard = ((None, a01, a02, a03), (None, a11, a12, a13))
-    fx, fy = {}, {}
-    for d in (1, 3, 2):
-        fx[d] = send(fo.at[:, pl.ds(0, 16)], heard[0][d], xdev(d), s1.at[0, d], r1.at[0, d])
-        fy[d] = send(fo.at[:, pl.ds(16, 16)], heard[1][d], ydev(d), s1.at[1, d], r1.at[1, d])
 
     for cp in ids:
         cp.wait()
@@ -137,6 +127,15 @@
     tab[...] = table
     tabr[0, y] = table
     tabr[1, x] = table
+    for cp in fcopies:
+        cp.wait()
+    pl.semaphore_wait(barrier, len(peers))
+
+    heard = ((None, a01, a02, a03), (None, a11, a12, a13))
+    fx, fy = {}, {}
+    for d in (1, 3, 2):
+        fx[d] = send(fo.at[:, pl.ds(0, 16)], heard[0][d], xdev(d), s1.at[0, d], r1.at[0, d])
+        fy[d] = send(fo.at[:, pl.ds(16, 16)], heard[1][d], ydev(d), s1.at[1, d], r1.at[1, d])
 
     tx = [send(tab, tabr.at[1, x], xdev(d), s1t.at[0, d], r1t.at[0, d]) for d in (1, 2, 3)]
     ty = [send(tab, tabr.at[0, y], ydev(d), s1t.at[1, d], r1t.at[1, d]) for d in (1, 2, 3)]
@@ -233,8 +232,8 @@
         wn[512 + 128 * g : 640 + 128 * g] = lo
 
     fz = [send(mv.at[z, c], mv.at[z, c], cdev, sf.at[0], rf.at[0])]
-    for i, d in enumerate(FAR):
-        mz[i].wait_recv()
+    for d in (2, 6, 1, 7, 3, 5, 4):
+        mz[FAR.index(d)].wait_recv()
         q = at_z(8 - d)
         fz.append(send(mv.at[q, c], mv.at[q, c], cdev, sf.at[d], rf.at[d]))
     for cp in cz:
@@ -275,7 +274,6 @@
         for i, j in PLANE
     ]
     gar[x, y] = wp[x, y]
-    oz = [send(oo.at[at_z(d)], orv.at[z], zdev(d), so.at[d], ro.at[d]) for d in FAR]
     orv[z] = oo[z]
 
     arrivals = {d: cp for d, cp in zip(FAR, gz)}
@@ -315,6 +313,8 @@
                 elif d:
                     to = qv.at[1, g, x]
                     back[h, g, d] = send(sb.at[1, g, d], to, xdev(d), sq.at[1, g, d], rq.at[1, g, d])
+
+    oz = [send(oo.at[at_z(d)], orv.at[z], zdev(d), so.at[d], ro.at[d]) for d in FAR]
 
     for cp in ga:
         cp.wait_recv()

time: 56.8 us -> 56.2 us (0.989)
  Pallas kernels: 55.8 us -> 54.9 us
    pallas_call x1, Pallas kernels: 54.1 us -> 53.2 us  [on_device(): pl.pallas_call(kernel, out_shape=(jax.ShapeDtypeStruct((32, 1024), F32),...]
where the time goes in v4:
time: 56.2 us; the launch traced here: 55.5 us
  Pallas kernels  54.9 us (98%)
  between operations  0.64 us (1%)
    pallas_call x1, Pallas kernels, on_device(): pl.pallas_call(kernel, out_shape=(jax.ShapeDtypeStruct((32, 1024), F32),...  53.2 us
    pallas_call x1, Pallas kernels, on_device(): pl.pallas_call(hand_over, out_shape=(jax.ShapeDtypeStruct((32, 1024), F32...  1.69 us

profile of v4, /device:TPU:2, one launch (start us, length us, event | category | flops | bytes accessed | tf_op | source)
XLA Modules:
  0.0 55.5 jit_solution(7668623432080818467)
XLA Ops:
  0.6 53.2 %graph_layer.1 = (f32[32,1024]{1,0:T(8,128)}, f32[32,1024]{1,0:T(8,128)}, f32[32,512]{1,0:T(8,128)}) custom-call(f32[32,1024]{1,0:T(8,128)} %feats.1, f32[32,512]{1,0:T(8,128)} %bitcast.2, f32[32,1024]{1,0:T(8,128)} %cot.1, f32[8,8,128,128]{3,2,1,0:T(8,128)} %tiles.1, s32[8,8]{1,0:T(8,128)} %cols_h.1, s32[8]{0:T(128)} %counts_h.1), custom_call_target="tpu_custom_call" | custom-call | flops 1000000000 | bytes 6000000 | tf_op jit(solution)/shard_map/graph_layer/pallas_call | solution.py:451
  53.8 1.7 %hand_over.1 = (f32[32,1024]{1,0:T(8,128)}, f32[32,1024]{1,0:T(8,128)}, f32[32,512]{1,0:T(8,128)}) custom-call(f32[32,1024]{1,0:T(8,128)} %get-tuple-element.9.a, f32[32,1024]{1,0:T(8,128)} %get-tuple-element.10.b, f32[32,512]{1,0:T(8,128)} %get-tuple-element.11.c), custom_call_target="tpu_custom_call" | custom-call | bytes 655360 | tf_op jit(solution)/shard_map/hand_over/pallas_call | solution.py:468

commit v5 on v4

--- a/solution.py
+++ b/solution.py
@@ -265,10 +265,10 @@
                 wp[a, g, q] = chunk
     xc.wait_recv()
     gz = []
-    gs[...] = pv[:, c] + px[...]
     for d in FAR:
+        gs[at_z(d)] = pv[at_z(d), c] + px[at_z(d)]
         gz.append(send(gs.at[at_z(d)], gv.at[z], zdev(d), sg.at[d], rg.at[d]))
-    gv[z] = gs[z]
+    gv[z] = pv[z, c] + px[z]
     ga = [
         send(wp.at[at_x(i), at_y(j)], gar.at[x, y], xydev(i, j), sga.at[i, j], rga.at[i, j])
         for i, j in PLANE
@@ -330,24 +330,29 @@
         for h in range(2):
             for d in (1, 3, 2):
                 back[h, g, d].wait_recv()
-            total = [jnp.zeros((16, 128), F32) for _ in range(8)]
-            for src in range(4):
-                for r in range(4):
-                    if h == 0:
-                        w = tabrs[0, src, 2, (at_x(g) * 4 + y) * 4 + r]
+            for part in range(2):
+                total = [jnp.zeros((16, 128), F32) for _ in range(4)]
+                for src in range(4):
+                    for r in range(4):
+                        if h == 0:
+                            w = tabrs[0, src, 2, (at_x(g) * 4 + y) * 4 + r]
+                        else:
+                            w = tabrs[1, src, 2, (x * 4 + at_y(g)) * 4 + r]
+                        piece = qv[h, g, src, r]
+                        for i in range(4):
+                            named = jnp.where(w == 4 * part + i, 1.0, 0.0).astype(F32)
+                            total[i] = total[i] + named * piece
+                for i in range(4):
+                    if g:
+                        dv[h, g, 4 * part + i] = total[i]
                     else:
-                        w = tabrs[1, src, 2, (x * 4 + at_y(g)) * 4 + r]
-                    piece = qv[h, g, src, r]
-                    for i in range(8):
-                        total[i] = total[i] + jnp.where(w == i, 1.0, 0.0).astype(F32) * piece
-            for i in range(8):
+                        ev[h, 0, 4 * part + i] = total[i]
                 if g:
-                    dv[h, g, i] = total[i]
-                else:
-                    ev[h, 0, i] = total[i]
-            if g:
-                device = ydev(g) if h else xdev(g)
-                last.append(send(dv.at[h, g], ev.at[h, g], device, se.at[h, g], re.at[h, g]))
+                    device = ydev(g) if h else xdev(g)
+                    piece = pl.ds(4 * part, 4)
+                    last.append(
+                        send(dv.at[h, g, piece], ev.at[h, g, piece], device, se.at[h, g, part], re.at[h, g, part])
+                    )
 
         if g == 1:
             for cp in gc:
@@ -445,7 +450,7 @@
         dma(8), dma(8), dma(8), dma(8), dma(8), dma(8), dma(8), dma(8),
         pltpu.SemaphoreType.DMA, pltpu.SemaphoreType.DMA,
         dma(8), dma(8), dma(8), dma(8), dma(8), dma(8),
-        dma(2, 4, 4), dma(2, 4, 4), dma(2, 4), dma(2, 4),
+        dma(2, 4, 4), dma(2, 4, 4), dma(2, 4, 2), dma(2, 4, 2),
         dma(4, 4), dma(4, 4), dma(4, 4), dma(4, 4),
     ]
     out, gf, gwt = pl.pallas_call(

time: 56.2 us -> 56.4 us (level)
  no operation moved by 1% of the time
where the time goes in v5:
time: 56.4 us; the launch traced here: 55.7 us
  Pallas kernels  55 us (98%)
  between operations  0.64 us (1%)
    pallas_call x1, Pallas kernels, on_device(): pl.pallas_call(kernel, out_shape=(jax.ShapeDtypeStruct((32, 1024), F32),...  53.3 us
    pallas_call x1, Pallas kernels, on_device(): pl.pallas_call(hand_over, out_shape=(jax.ShapeDtypeStruct((32, 1024), F32...  1.69 us

profile of v5, /device:TPU:2, one launch (start us, length us, event | category | flops | bytes accessed | tf_op | source)
XLA Modules:
  0.0 55.7 jit_solution(10660754052244800474)
XLA Ops:
  0.6 53.3 %graph_layer.1 = (f32[32,1024]{1,0:T(8,128)}, f32[32,1024]{1,0:T(8,128)}, f32[32,512]{1,0:T(8,128)}) custom-call(f32[32,1024]{1,0:T(8,128)} %feats.1, f32[32,512]{1,0:T(8,128)} %bitcast.2, f32[32,1024]{1,0:T(8,128)} %cot.1, f32[8,8,128,128]{3,2,1,0:T(8,128)} %tiles.1, s32[8,8]{1,0:T(8,128)} %cols_h.1, s32[8]{0:T(128)} %counts_h.1), custom_call_target="tpu_custom_call" | custom-call | flops 1000000000 | bytes 6000000 | tf_op jit(solution)/shard_map/graph_layer/pallas_call | solution.py:456
  54.0 1.7 %hand_over.1 = (f32[32,1024]{1,0:T(8,128)}, f32[32,1024]{1,0:T(8,128)}, f32[32,512]{1,0:T(8,128)}) custom-call(f32[32,1024]{1,0:T(8,128)} %get-tuple-element.9.a, f32[32,1024]{1,0:T(8,128)} %get-tuple-element.10.b, f32[32,512]{1,0:T(8,128)} %get-tuple-element.11.c), custom_call_target="tpu_custom_call" | custom-call | bytes 655360 | tf_op jit(solution)/shard_map/hand_over/pallas_call | solution.py:473
